TPU v7x, 256 devices: a whole 4x4x8 slice. The times are simulated.
256 devices in a mesh: ctx: 16 (over y, x), head: 16 (over z, core).
Axes of the slice: x: 4, y: 4, z: 8, core: 2. Of those that a mesh axis runs over, the one named last changes fastest.
Arguments:
- queries: bfloat16 [2048, 24576], P(('ctx', 'head')), may hold values from -400 to 400
- cache_latent: bfloat16 [1024, 64, 512], P('ctx'), may hold values from -6 to 6
- cache_rope: bfloat16 [1024, 4096], P('ctx'), may hold values from -6 to 6
- selected: int32 [32, 32], replicated, may hold values from 0 to 1023, as said below
- w_uk: bfloat16 [128, 128, 512], P('head'), may hold values from -0.5 to 0.5
- value_up_weight: bfloat16 [128, 512, 128], P('head'), may hold values from -0.25 to 0.25
Outputs:
- attended: bfloat16 [2048, 128, 128], P('ctx', 'head')
Inputs may be any that keep to these rules, and one draw needn't show every extreme that they name: `selected`: in each row the 32 block numbers are distinct; at most 4 of them share the value of number // 64, and in every row some value is shared by exactly 4.
All inputs are finite; a program needn't handle non-finite values.
Results may differ from a plain program's by a relative error of at most 0.014.
Values may be sent and summed in bfloat16 or wider, within the bound.
A program may use at most 192 MiB of HBM per device.

v0:
```python
import math

import jax
import jax.numpy as jnp
from jax import lax
from jax.sharding import PartitionSpec as P

NOPE = 128
ROPE = 64
KVL = 512
VHD = 128
BLK = 64


def build_slots(selected, shards, per_shard, shard_most):
    owner_id = selected // per_shard
    offset = selected % per_shard
    pick_count = selected.shape[1]
    same_owner = owner_id[:, :, None] == owner_id[:, None, :]
    before = jnp.arange(pick_count)[:, None] > jnp.arange(pick_count)[None, :]
    rank_in_owner = jnp.sum(jnp.logical_and(same_owner, before[None]).astype(jnp.int32), axis=2)
    slot_hit = jnp.logical_and(
        owner_id[:, :, None, None] == jnp.arange(shards)[None, None, :, None],
        rank_in_owner[:, :, None, None] == jnp.arange(shard_most)[None, None, None, :],
    )
    return jnp.sum(jnp.where(slot_hit, offset[:, :, None, None] + 1, 0), axis=1) - 1


def score_rows(block_latent, block_rope, latent_rows, rope_rows):
    score_scale = 1.0 / math.sqrt(NOPE + ROPE)
    from_latent = jnp.einsum(
        "rhk,tk->rht", block_latent, latent_rows, preferred_element_type=jnp.float32
    )
    from_rope = jnp.einsum("rhe,te->rht", block_rope, rope_rows, preferred_element_type=jnp.float32)
    return (from_latent + from_rope) * score_scale


def value_mix(weights, latent_rows, value_up_weight):
    blended_latent_rows = jnp.einsum(
        "rht,tk->rhk", weights.astype(jnp.bfloat16), latent_rows, preferred_element_type=jnp.float32
    )
    upper_half_slice = blended_latent_rows.astype(jnp.bfloat16)
    lower_half_slice = (blended_latent_rows - upper_half_slice.astype(jnp.float32)).astype(
        jnp.bfloat16
    )
    upper_half_output = jnp.einsum(
        "diz,izw->diw", upper_half_slice, value_up_weight, preferred_element_type=jnp.float32
    )
    lower_half_output = jnp.einsum(
        "diz,izw->diw", lower_half_slice, value_up_weight, preferred_element_type=jnp.float32
    )
    return upper_half_output + lower_half_output


def local(queries, cache_latent, cache_rope, selected, w_uk, value_up_weight):
    head_count = w_uk.shape[0]
    shards = lax.axis_size("ctx")
    own_index = lax.axis_index("ctx")
    regrouped = lax.all_to_all(queries, "head", split_axis=1, concat_axis=0, tiled=True)
    row_count = regrouped.shape[0]
    split_heads = regrouped.reshape(row_count, head_count, NOPE + ROPE)
    latent_query = jnp.einsum(
        "rhn,hnk->rhk", split_heads[:, :, :NOPE], w_uk, preferred_element_type=jnp.float32
    ).astype(jnp.bfloat16)
    rope_query = split_heads[:, :, NOPE:]
    per_shard = cache_latent.shape[0]
    shard_most = 2 * selected.shape[1] // shards
    slots = build_slots(selected, shards, per_shard, shard_most)
    own_column = lax.dynamic_index_in_dim(slots, own_index, 1, keepdims=False)
    every_latent, every_rope = (
        lax.all_gather(latent_query, "ctx", axis=0, tiled=True),
        lax.all_gather(rope_query, "ctx", axis=0, tiled=True),
    )
    all_rows = every_latent.shape[0]
    blocks_all = all_rows // BLK
    wanted = jnp.maximum(own_column, 0)
    latent_here = cache_latent[wanted].reshape(blocks_all, -1, KVL)
    rope_here = cache_rope[wanted].reshape(blocks_all, -1, ROPE)
    keep_mask = jnp.repeat(own_column >= 0, BLK, axis=1)

    def score_block(inputs):
        block_latent, block_rope, latent_part, rope_part, keep_part = inputs
        scores = score_rows(block_latent, block_rope, latent_part, rope_part)
        return jnp.where(keep_part[None, None, :], scores, -1e30)

    scores = lax.map(
        score_block,
        (
            every_latent.reshape(blocks_all, BLK, head_count, KVL),
            every_rope.reshape(blocks_all, BLK, head_count, ROPE),
            latent_here,
            rope_here,
            keep_mask,
        ),
    )
    local_top = jnp.max(scores, axis=3)
    row_top = lax.pmax(local_top.astype(jnp.bfloat16), "ctx").astype(local_top.dtype)

    def mix_block(inputs):
        block_scores, block_top, latent_part, keep_part = inputs
        weights = jnp.where(
            keep_part[None, None, :], jnp.exp(block_scores - block_top[:, :, None]), 0.0
        )
        return (value_mix(weights, latent_part, value_up_weight), jnp.sum(weights, axis=2))

    partial_values, partial_totals = lax.map(mix_block, (scores, row_top, latent_here, keep_mask))
    values_mine, totals_mine = (
        lax.psum_scatter(
            partial_values.reshape(all_rows, head_count, VHD),
            "ctx",
            scatter_dimension=0,
            tiled=True,
        ),
        lax.psum_scatter(
            partial_totals.reshape(all_rows, head_count), "ctx", scatter_dimension=0, tiled=True
        ),
    )
    return (values_mine / totals_mine[:, :, None]).astype(jnp.bfloat16)


def solution(mesh):
    placed = (
        P(("ctx", "head"), None),
        P("ctx", None, None),
        P("ctx", None),
        P(),
        P("head", None, None),
        P("head", None, None),
    )
    return jax.shard_map(
        local, mesh=mesh, in_specs=placed, out_specs=P("ctx", "head", None), check_vma=False
    )
```

profile of v0, /device:TPU:1, one launch (start us, length us, event | category | flops | bytes accessed | tf_op | source)
XLA Modules:
  0.0 765.1 jit_solution(17080982288405627276)
XLA Ops:
  6.5 24.7 %all_to_all.16 = bf16[8,16,1536]{2,0,1:T(8,128)(2,1)S(1)} all-to-all(bf16[8,16,1536]{2,0,1:T(8,128)(2,1)} %bitcast.90), channel_id=1, replica_groups=mesh['ctx'=16,'head'=16] {'head'}, dimensions={1} | all-to-all | bytes 786432 | tf_op jit(solution)/shard_map/all_to_all | solution.py:59
  32.6 1.5 fusion.32
  35.8 2.3 select_reduce_fusion
  38.9 8.7 %gather_fusion = bf16[128,64,512]{2,1,0:T(8,128)(2,1)} fusion(bf16[64,64,512]{2,1,0:T(8,128)(2,1)} %param.11, s32[1024]{0:T(1024)S(1)} %pad_clamp_fusion), kind=kCustom, calls=%fused_computation | custom fusion | bytes 16777728 | tf_op jit(solution)/shard_map/gather | solution.py:77
  47.7 2.2 gather_fusion.1
  49.8 3.3 reshape.87
  53.1 1.6 copy.49
  55.3 25.8 %all-gather.5.cloned.1.call-done = bf16[2048,8,64]{0,2,1:T(8,128)(2,1)} async-done(((bf16[128,8,64]{0,2,1:T(8,128)(2,1)}), bf16[2048,8,64]{0,2,1:T(8,128)(2,1)}) %all-gather.5.cloned.1.call-update) | async-done | bytes 2097168 | tf_op jit(solution)/shard_map/all_gather | solution.py:72
  81.1 5.6 copy.54
  86.8 122.3 %all-gather.3.cloned.1.call-done = bf16[2048,8,512]{0,2,1:T(8,128)(2,1)} async-done(((bf16[128,8,512]{0,2,1:T(8,128)(2,1)}), bf16[2048,8,512]{0,2,1:T(8,128)(2,1)}) %all-gather.3.cloned.1.call-update) | async-done | bytes 16777232 | tf_op jit(solution)/shard_map/all_gather | solution.py:71
  209.1 23.9 %copy.46 = bf16[2048,8,512]{2,1,0:T(8,128)(2,1)} copy(bf16[2048,8,512]{0,2,1:T(8,128)(2,1)} %all-gather.3.cloned.1.call-done) | data formatting | bytes 33554432 | tf_op jit(solution)/shard_map/all_gather | solution.py:71
  233.0 109.1 %while.22 = (s32[]{:T(128)}, f32[32,64,8,256]{3,2,1,0:T(8,128)}, pred[32,256]{1,0:T(8,128)(4,1)S(1)}, bf16[32,64,8,512]{3,2,1,0:T(8,128)(2,1)}, bf16[32,256,512]...) while((s32[]{:T(128)}, f32[32,64,8,256]{3,2,1,0:T(8,128)}, ...), condition=%wide.region_3.4_spmd, body=%wide.region_2.3_spmd.sunk | while | flops 151388160 | bytes 2526553 | solution.py:86
  234.4 1.9 fusion.59
  237.8 1.9 fusion.59
  241.2 1.9 fusion.59
  244.7 1.9 fusion.59
  248.1 1.9 fusion.59
  251.5 1.9 fusion.59
  254.9 1.9 fusion.59
  258.3 1.9 fusion.59
  261.7 1.9 fusion.59
  265.1 1.9 fusion.59
  268.5 1.9 fusion.59
  271.9 1.9 fusion.59
  275.3 1.9 fusion.59
  278.7 1.9 fusion.59
  282.1 1.9 fusion.59
  285.5 1.9 fusion.59
  288.9 2.0 fusion.59
  292.4 2.0 fusion.59
  295.8 1.9 fusion.59
  299.2 1.9 fusion.59
  302.6 2.0 fusion.59
  306.0 1.9 fusion.59
  309.5 1.9 fusion.59
  312.8 1.9 fusion.59
  316.3 1.9 fusion.59
  319.7 2.0 fusion.59
  323.1 1.9 fusion.59
  326.5 1.9 fusion.59
  329.9 1.9 fusion.59
  333.3 1.9 fusion.59
  336.7 1.9 fusion.59
  340.1 1.9 fusion.59
  342.0 8.2 %reduce_max.9 = bf16[32,64,8]{2,1,0:T(8,128)(2,1)S(1)} reduce(f32[32,64,8,256]{3,2,1,0:T(8,128)} %get-tuple-element.274, bf16[]{:T(256)} %constant.143), dimensions={3}, to_apply=%region_4.5 | reduce | flops 4177920 | bytes 16809986 | tf_op jit(solution)/shard_map/reduce_max | solution.py:96
  350.2 64.3 %pmax.7 = bf16[32,64,8]{2,1,0:T(8,128)(2,1)S(1)} all-reduce(bf16[32,64,8]{2,1,0:T(8,128)(2,1)S(1)} %reduce_max.9), channel_id=1, replica_groups=mesh['ctx'=16,'head'=16] {'ctx'}, use_global_device_ids=true, to_apply=%region_5.6 | all-reduce | flops 16384 | bytes 65536 | tf_op jit(solution)/shard_map/pmax | solution.py:97
  414.7 160.3 %while.23 = (s32[]{:T(128)}, f32[32,64,8,128]{3,2,1,0:T(8,128)}, f32[32,64,8]{2,1,0:T(8,128)}, pred[32,256]{1,0:T(8,128)(4,1)S(1)}, f32[32,64,8,256]{3,2,1,0:T(8...) while((s32[]{:T(128)}, f32[32,64,8,128]{3,2,1,0:T(8,128)}, ...), condition=%wide.region_8.9_spmd, body=%wide.region_6.8_spmd.sunk | while | flops 270335488 | bytes 6863977 | solution.py:106
  414.8 1.5 subtract_convert_fusion.2
  429.8 1.5 subtract_convert_fusion.2
  434.8 1.5 subtract_convert_fusion.2
  459.8 1.5 subtract_convert_fusion.2
  464.8 1.5 subtract_convert_fusion.2
  484.9 1.5 subtract_convert_fusion.2
  494.9 1.5 subtract_convert_fusion.2
  499.9 1.5 subtract_convert_fusion.2
  504.8 1.5 subtract_convert_fusion.2
  529.9 1.5 subtract_convert_fusion.2
  554.9 1.5 subtract_convert_fusion.2
  564.9 1.5 subtract_convert_fusion.2
  570.0 1.5 subtract_convert_fusion.2
  574.9 2.2 copy.55
  577.8 85.0 %reduce-scatter.5.cloned.1.call-done = f32[128,8]{0,1:T(8,128)} async-done(((f32[2048,8]{0,1:T(8,128)}), f32[128,8]{0,1:T(8,128)}) %reduce-scatter.5.cloned.1.call-update) | async-done | bytes 4112 | tf_op jit(solution)/shard_map/reduce_scatter | solution.py:114
  663.5 93.1 %reduce-scatter.3.cloned.1.call-done = f32[128,8,128]{2,1,0:T(8,128)} async-done(((f32[2048,8,128]{2,1,0:T(8,128)}), f32[128,8,128]{2,1,0:T(8,128)}) %reduce-scatter.3.cloned.1.call-update) | async-done | bytes 524304 | tf_op jit(solution)/shard_map/reduce_scatter | solution.py:108
  756.7 2.0 divide_convert_fusion
  (345 shorter events, 193.3 us)
Async XLA Ops:
  6.5 26.1 %copy-start = (bf16[8,128,512]{2,1,0:T(8,128)(2,1)S(1)}, bf16[8,128,512]{2,1,0:T(8,128)(2,1)}, u32[]{:S(2)}) copy-start(bf16[8,128,512]{2,1,0:T(8,128)(2,1)} %param.14) | copy-start | bytes 3145732
  6.5 74.6 %all-gather.5.cloned.1.call-start = ((), (), s32[]{:S(2)}) async-start(), calls=%async_computation.4 | async-start | bytes 2228224 | tf_op jit(solution)/shard_map/all_gather | solution.py:72
  32.5 176.6 %all-gather.3.cloned.1.call-start = ((), (), s32[]{:S(2)}) async-start(), calls=%async_computation.3 | async-start | bytes 17825792 | tf_op jit(solution)/shard_map/all_gather | solution.py:71
  34.1 628.6 %reduce-scatter.5.cloned.1.call-start = ((), (), s32[]{:S(2)}) async-start(), calls=%async_computation.6 | async-start | bytes 69632 | tf_op jit(solution)/shard_map/reduce_scatter | solution.py:114
  38.9 8.7 %copy-start.2 = (bf16[64,4096]{1,0:T(8,128)(2,1)S(1)}, bf16[64,4096]{1,0:T(8,128)(2,1)}, u32[]{:S(2)}) copy-start(bf16[64,4096]{1,0:T(8,128)(2,1)} %param.12) | copy-start | bytes 1572868
  342.0 72.7 %copy-start.3 = (bf16[8,512,128]{2,1,0:T(8,128)(2,1)S(1)}, bf16[8,512,128]{2,1,0:T(8,128)(2,1)}, u32[]{:S(2)}) copy-start(bf16[8,512,128]{2,1,0:T(8,128)(2,1)} %param.15) | copy-start | bytes 3145732
  574.9 183.7 %copy-start.1 = (bf16[8,128,512]{2,1,0:T(8,128)(2,1)S(1)}, bf16[8,128,512]{2,1,0:T(8,128)(2,1)}, u32[]{:S(2)}) copy-start(bf16[8,128,512]{2,1,0:T(8,128)(2,1)} %param.14) | copy-start | bytes 3145732
  577.2 179.4 %reduce-scatter.3.cloned.1.call-start = ((), (), s32[]{:S(2)}) async-start(), calls=%async_computation.5 | async-start | bytes 8912896 | tf_op jit(solution)/shard_map/reduce_scatter | solution.py:108
Sparse Core Ops, SparseCore 0:
  32.6 48.4 all-gather.4
  83.5 125.4 all-gather.2
  577.3 85.3 reduce-scatter.4
  666.8 89.8 reduce-scatter.2
where the time goes:
time: 770 us; the launch traced here: 765 us
  waiting for transfers between devices  327 us (42%)
  matrix products  180 us (23%)
  local copies, waits for them, and re-layouts  99.3 us (13%)
  blocking collectives  89 us (12%)
  other arithmetic  55.6 us (7%)
  between operations  13.3 us (2%)
    all_gather x1, waiting for transfers between devices, local(): lax.all_gather(latent_query, 'ctx', axis=0, tiled=True)  122 us
    reduce_scatter x1, waiting for transfers between devices, local(): lax.psum_scatter(partial_values.reshape(all_rows, head_count, VHD), 'ctx'...  93.1 us
    reduce_scatter x1, waiting for transfers between devices, local(): lax.psum_scatter(partial_totals.reshape(all_rows, head_count), 'ctx', sca...  85 us
    pmax x1, blocking collectives, local(): lax.pmax(local_top.astype(jnp.bfloat16), 'ctx').astype(local_top.dtype)  64.3 us
    dot_general x32, matrix products, score_rows(): jnp.einsum('rhe,te->rht', block_rope, rope_rows, preferred_element_type=j...  61.8 us
    dynamic_update_slice x64, local copies, waits for them, and re-layouts, local(): lax.map(mix_block, (scores, row_top, latent_here, keep_mask))  47.3 us
    dot_general x32, matrix products, value_mix(): jnp.einsum('rht,tk->rhk', weights.astype(jnp.bfloat16), latent_rows, pref...  46.8 us
    dot_general x32, matrix products, score_rows(): jnp.einsum('rhk,tk->rht', block_latent, latent_rows, preferred_element_ty...  46.1 us
  transfers between devices with their start and end apart: 4, of which 4 were waited for; matrix products, arithmetic and copies ran while one was open for 4% of the time, Pallas kernels for 0%

commit v1 on v0

v1 whole, which is shorter than its diff:
```python
import functools
import math

import jax
import jax.numpy as jnp
from jax import lax
from jax.experimental import pallas as pl
from jax.experimental.pallas import tpu as pltpu
from jax.sharding import PartitionSpec as P

NOPE = 128
ROPE = 64
KVL = 512
VHD = 128
BLK = 64
HALF = KVL // 2
N_CTX = 16
N_HEAD = 16
HEADS = 8
HEAD_COLS = HEADS * (NOPE + ROPE)
SLOT = 144
CLASSES = 8
PICKS = 8
MESH = pl.DeviceIdType.MESH
DIRECT = (0, 4, 3)
RING_STEPS = 2
SUBS = 2
SUB = PICKS // SUBS
NT = (((1,), (1,)), ((), ()))
ROW_TILE = 256
SCALE = math.log2(math.e) / math.sqrt(NOPE + ROPE)


def kernel(
    q_hbm,
    cache_hbm,
    rope_hbm,
    sel_hbm,
    w_hbm,
    v_hbm,
    out,
    sel_v,
    rank_v,
    tab_v,
    tab,
    out_wide,
    cache_v,
    rope_land,
    rope_wide,
    rope_v,
    rope_keys,
    w_v,
    v_v,
    q_land,
    q_all,
    acc,
    top,
    total,
    g_mine,
    g_other,
    *rest,
):
    nd = len(DIRECT)
    send_bufs, recv_bufs = rest[:nd], rest[nd : 2 * nd]
    (
        local_sem,
        q_send,
        q_recv,
        xy_send,
        xy_recv,
        ring_send,
        ring_recv,
        last_send,
        last_recv,
        core_send,
        core_recv,
    ) = rest[2 * nd :]
    ctx = lax.axis_index("ctx")
    head = lax.axis_index("head")
    z = lax.div(head, 2)
    core = lax.rem(head, 2)

    def direct(d):
        return DIRECT[d] + 2 * core if d == 2 else DIRECT[d]

    def local_copies():
        mine = pl.multiple_of(core * HALF, HALF)
        other = pl.multiple_of(HALF - core * HALF, HALF)
        cols = pl.ds(pl.multiple_of(head * HEAD_COLS, 128), HEAD_COLS)
        return [
            pltpu.make_async_copy(
                cache_hbm.at[:, :, pl.ds(mine, HALF)], cache_v, local_sem.at[0]
            ),
            pltpu.make_async_copy(
                rope_hbm.at[:, pl.ds(pl.multiple_of(core * 2048, 2048), 2048)],
                rope_land,
                local_sem.at[1],
            ),
            pltpu.make_async_copy(q_hbm.at[:, cols], q_land.at[:, cols], local_sem.at[2]),
            pltpu.make_async_copy(
                w_hbm.at[:, :, pl.ds(mine, HALF)], w_v.at[:, :, pl.ds(0, HALF)], local_sem.at[3]
            ),
            pltpu.make_async_copy(
                w_hbm.at[:, :, pl.ds(other, HALF)],
                w_v.at[:, :, pl.ds(HALF, HALF)],
                local_sem.at[4],
            ),
            pltpu.make_async_copy(
                v_hbm.at[:, pl.ds(mine, HALF)], v_v.at[:, pl.ds(0, HALF)], local_sem.at[5]
            ),
            pltpu.make_async_copy(
                v_hbm.at[:, pl.ds(other, HALF)], v_v.at[:, pl.ds(HALF, HALF)], local_sem.at[6]
            ),
            pltpu.make_async_copy(sel_hbm, sel_v, local_sem.at[7]),
        ]

    copies = local_copies()
    for place in (7, 0, 1, 2, 3, 4, 5, 6):
        copies[place].start()

    barrier = pltpu.get_barrier_semaphore()

    @pl.loop(1, N_CTX)
    def _(i):
        pl.semaphore_signal(
            barrier,
            inc=1,
            device_id={"ctx": lax.rem(ctx + i, N_CTX), "head": head},
            device_id_type=MESH,
        )
        pl.semaphore_signal(
            barrier,
            inc=1,
            device_id={"ctx": ctx, "head": lax.rem(head + i, N_HEAD)},
            device_id_type=MESH,
        )

    copies[7].wait()
    sel = sel_v[...]
    rank = jnp.zeros_like(sel)
    for j in range(32):
        rank += (sel[:, j : j + 1] < sel).astype(jnp.int32)
    mine = lax.shift_right_logical(sel, 6) == ctx
    tab_v[...] = jnp.zeros_like(tab_v)
    for m in range(4):
        here = jnp.logical_and(mine, (rank & 3) == m)
        block = jnp.sum(jnp.where(here, sel & 63, 0), axis=1, keepdims=True)
        tab_v[0:32, m : m + 1] = block
    rank_v[...] = rank
    own_rank = rank_v[pl.ds(2 * ctx, 2), :]
    own_from = lax.shift_right_logical(sel_v[pl.ds(2 * ctx, 2), :], 6)
    position = lax.broadcasted_iota(jnp.int32, (2, 32), 1)
    source = jnp.zeros((2, 32), jnp.int32)
    for j in range(32):
        source += jnp.where(position == own_rank[:, j : j + 1], own_from[:, j : j + 1], 0)
    tab_v[32:34, 0:32] = source
    tab_copy = pltpu.make_async_copy(tab_v, tab, local_sem.at[8])
    tab_copy.start()

    def q_copy(i):
        to = lax.rem(head + i, N_HEAD)
        return pltpu.make_async_remote_copy(
            src_ref=q_hbm.at[:, pl.ds(pl.multiple_of(to * HEAD_COLS, 128), HEAD_COLS)],
            dst_ref=q_land.at[:, pl.ds(pl.multiple_of(head * HEAD_COLS, 128), HEAD_COLS)],
            send_sem=q_send.at[i],
            recv_sem=q_recv.at[i],
            device_id={"ctx": ctx, "head": to},
            device_id_type=MESH,
        )

    def xy_copy(d, i):
        return pltpu.make_async_remote_copy(
            src_ref=send_bufs[d].at[i],
            dst_ref=recv_bufs[d].at[ctx],
            send_sem=xy_send.at[d, i],
            recv_sem=xy_recv.at[d, i],
            device_id={"ctx": lax.rem(ctx + i, N_CTX), "head": head},
            device_id_type=MESH,
        )

    def picked(d, to):
        group = lax.rem(z + direct(d), CLASSES)
        block = tab[2 * to + lax.div(group, 4), lax.rem(group, 4)]
        return cache_v[block], rope_v[block]

    def stage(d):
        @pl.loop(1, N_CTX, unroll=5)
        def _(i):
            latent, rope = picked(d, lax.rem(ctx + i, N_CTX))
            send_bufs[d][i, 0:64, :] = latent[:, :128]
            send_bufs[d][i, 64:128, :] = latent[:, 128:]
            send_bufs[d][i, 128:144, :] = rope

        latent, rope = picked(d, ctx)
        recv_bufs[d][ctx, 0:64, :] = latent[:, :128]
        recv_bufs[d][ctx, 64:128, :] = latent[:, 128:]
        recv_bufs[d][ctx, 128:144, :] = rope

    def give(d):
        @pl.loop(1, N_CTX, unroll=5)
        def _(i):
            xy_copy(d, i).start()

    pl.semaphore_wait(barrier, 2 * (N_CTX - 1))

    @pl.loop(1, N_HEAD)
    def _(i):
        q_copy(i).start()

    copies[1].wait()
    for i in range(16):
        rope_wide[pl.ds(i, 64, stride=16), :] = rope_land[:, i * 128 : i * 128 + 128].astype(
            jnp.float32
        )
    rope_v[...] = rope_wide[...].astype(jnp.bfloat16).reshape(64, 16, 128)
    copies[0].wait()
    tab_copy.wait()
    stage(0)
    give(0)
    for d in range(1, nd):
        stage(d)

    acc[...] = jnp.zeros_like(acc)
    total[...] = jnp.zeros_like(total)
    top[...] = jnp.full_like(top, -1e30)

    def ring_copy(direction, step, sub):
        source = (CLASSES - step) % CLASSES if direction == 0 else step
        target = CLASSES - step - 1 if direction == 0 else step + 1
        to = lax.rem(head + (2 if direction == 0 else N_HEAD - 2), N_HEAD)
        part = pl.ds(sub * SUB, SUB)
        return pltpu.make_async_remote_copy(
            src_ref=g_mine.at[source, part],
            dst_ref=g_mine.at[target, part],
            send_sem=ring_send.at[direction, step, sub],
            recv_sem=ring_recv.at[direction, step, sub],
            device_id={"ctx": ctx, "head": to},
            device_id_type=MESH,
        )

    last = 5 - 2 * core

    def last_copy(sub):
        part = pl.ds(sub * SUB, SUB)
        return pltpu.make_async_remote_copy(
            src_ref=g_mine.at[6 - 4 * core, part],
            dst_ref=g_mine.at[last, part],
            send_sem=last_send.at[sub],
            recv_sem=last_recv.at[sub],
            device_id={"ctx": ctx, "head": lax.rem(head + 2 + (N_HEAD - 4) * core, N_HEAD)},
            device_id_type=MESH,
        )

    def core_copy(rel, sub):
        part = pl.ds(sub * SUB, SUB)
        return pltpu.make_async_remote_copy(
            src_ref=g_mine.at[rel, part],
            dst_ref=g_other.at[rel, part],
            send_sem=core_send.at[rel, sub],
            recv_sem=core_recv.at[rel, sub],
            device_id={"ctx": ctx, "head": head + 1 - 2 * core},
            device_id_type=MESH,
        )

    def share(rel):
        for sub in range(SUBS):
            core_copy(rel, sub).start()

    def take(d):
        @pl.loop(1, 12)
        def _(i):
            xy_copy(d, i).wait_recv()

        if d == 0:
            give(1)

        @pl.loop(12, N_CTX)
        def _(i):
            xy_copy(d, i).wait_recv()

        rel = direct(d)
        group = lax.rem(z + rel, CLASSES)
        row = 32 + lax.div(group, 4)
        for j in range(PICKS):
            g_mine[rel, j] = recv_bufs[d][tab[row, lax.rem(group, 4) + 4 * j]]

    def load(rel, first, count, place):
        picks = pl.ds(first, count)
        latent = jnp.concatenate(
            [
                g_mine[rel, picks, 0:64, :],
                g_mine[rel, picks, 64:128, :],
                g_other[rel, picks, 0:64, :],
                g_other[rel, picks, 64:128, :],
            ],
            axis=2,
        ).reshape(count * BLK, KVL)
        lane_low = lax.broadcasted_iota(jnp.int32, (count, 16, 128), 2) < 64
        for held, half in ((g_mine, core), (g_other, 1 - core)):
            pairs = held[rel, picks, 128:144, :].astype(jnp.float32)
            zero = jnp.zeros_like(pairs)
            even = pl.ds(32 * half, 16, stride=2)
            odd = pl.ds(32 * half + 1, 16, stride=2)
            rope_keys[place, 0:count, even, :] = jnp.where(lane_low, pairs, zero)
            rope_keys[place, 0:count, odd, :] = jnp.where(lane_low, zero, pairs)
        rope = rope_keys[place, 0:count].astype(jnp.bfloat16).reshape(count * BLK, 128)
        return latent, jnp.concatenate([latent, rope], axis=1)

    def attend(*items):
        for rel, first, count in items:
            for sub in range(first // SUB, (first + count) // SUB):
                core_copy(rel, sub).wait_recv()
        units = []
        for place, (rel, first, count) in enumerate(items):
            b = lax.div(lax.rem(z + rel, CLASSES), 4)
            latent, keys = load(rel, first, count, place)
            for tile in range(512 // ROW_TILE):
                units.append((b, pl.ds(tile * ROW_TILE, ROW_TILE), latent, keys))

        def score_unit(b, rows, _, keys):
            return lax.dot_general(q_all[b, rows, :], keys, NT, preferred_element_type=jnp.float32)

        score = score_unit(*units[0])
        for place, (b, rows, latent, keys) in enumerate(units):
            later = score_unit(*units[place + 1]) if place + 1 < len(units) else None
            before = top[b, rows, :]
            now = jnp.maximum(before, jnp.max(score, axis=1, keepdims=True))
            fade = jnp.exp2((before - now) * SCALE)
            parts = [
                jnp.exp2((score[:, c * 128 : c * 128 + 128] - now) * SCALE)
                for c in range(score.shape[1] // 128)
            ]
            top[b, rows, :] = now
            total[b, rows, :] = total[b, rows, :] * fade + sum(parts[1:], parts[0])
            weights = jnp.concatenate(parts, axis=1).astype(jnp.bfloat16)
            mixed = jnp.dot(weights, latent, preferred_element_type=jnp.float32)
            for c in range(4):
                cols = slice(c * 128, c * 128 + 128)
                acc[b, rows, cols] = acc[b, rows, cols] * fade + mixed[:, cols]
            score = later

    def forward(step, sub):
        for direction in range(2):
            ring_copy(direction, step, sub).wait_recv()
            if step + 1 < RING_STEPS:
                ring_copy(direction, step + 1, sub).start()
        if step + 1 == RING_STEPS:
            last_copy(sub).start()
        for rel in (CLASSES - step - 1, step + 1):
            core_copy(rel, sub).start()

    def end(sub):
        last_copy(sub).wait_recv()
        core_copy(last, sub).start()

    def absorb():
        copies[2].wait()

        @pl.loop(1, N_HEAD)
        def _(i):
            q_copy(i).wait_recv()

        copies[3].wait()
        copies[4].wait()
        low = lax.broadcasted_iota(jnp.int32, (8 * N_HEAD, 128), 1) < 64
        for pair in range(HEADS // 2):
            tiles = []
            for t in range(3):
                column = pair * 384 + t * 128
                tiles.append(
                    jnp.concatenate(
                        [
                            q_land[:, h * HEAD_COLS + column : h * HEAD_COLS + column + 128].astype(
                                jnp.float32
                            )
                            for h in range(N_HEAD)
                        ],
                        axis=0,
                    )
                )
            swap1 = pltpu.roll(tiles[1], 64, 1)
            swap2 = pltpu.roll(tiles[2], 64, 1)
            nopes = (tiles[0], jnp.where(low, swap1, swap2))
            ropes = (jnp.where(low, tiles[1], swap1), jnp.where(low, swap2, tiles[2]))
            for parity in range(2):
                n = 2 * pair + parity
                absorbed = jnp.dot(
                    nopes[parity].astype(jnp.bfloat16), w_v[n], preferred_element_type=jnp.float32
                ).astype(jnp.bfloat16)
                rope = ropes[parity].astype(jnp.bfloat16)
                for b in range(2):
                    q_all[b, n * 64 : n * 64 + 64, 0:KVL] = absorbed[b * 64 : b * 64 + 64]
                    q_all[b, n * 64 : n * 64 + 64, KVL:] = rope[b * 64 : b * 64 + 64]

    take(0)
    for sub in range(SUBS):
        for direction in range(2):
            ring_copy(direction, 0, sub).start()
    share(0)
    give(2)
    absorb()
    attend((0, 0, PICKS))
    forward(0, 0)
    attend((7, 0, SUB), (1, 0, SUB))
    forward(0, 1)
    take(1)
    share(4)
    attend((7, SUB, SUB), (1, SUB, SUB))
    forward(1, 0)
    attend((4, 0, PICKS), (6, 0, SUB), (2, 0, SUB))
    forward(1, 1)
    take(2)
    share(direct(2))
    attend((6, SUB, SUB), (2, SUB, SUB))
    end(0)
    attend((direct(2), 0, SUB), (last, 0, SUB))
    end(1)
    attend((direct(2), SUB, SUB), (last, SUB, SUB))

    copies[5].wait()
    copies[6].wait()
    for n in range(HEADS):
        rows = slice(n * 64, n * 64 + 64)
        mixed = acc[:, rows, :].reshape(128, KVL).astype(jnp.bfloat16)
        value = jnp.dot(mixed, v_v[n], preferred_element_type=jnp.float32)
        sums = jnp.sum(total[:, rows, :].reshape(128, 128), axis=1, keepdims=True)
        out_wide[pl.ds(n, 128, stride=HEADS), :] = value / sums
    out[...] = out_wide[...].astype(jnp.bfloat16).reshape(128, HEADS, VHD)

    @pl.loop(1, N_HEAD)
    def _(i):
        q_copy(i).wait_send()
        for d in range(nd):
            xy_copy(d, i).wait_send()

    for step in range(RING_STEPS):
        for sub in range(SUBS):
            for direction in range(2):
                ring_copy(direction, step, sub).wait_send()
    for sub in range(SUBS):
        last_copy(sub).wait_send()
        for rel in range(CLASSES):
            core_copy(rel, sub).wait_send()


def local(queries, cache_latent, cache_rope, selected, w_uk, value_up_weight):
    bf16 = jnp.bfloat16
    nd = len(DIRECT)
    dma = pltpu.SemaphoreType.DMA
    any_spec = pl.BlockSpec(memory_space=pl.ANY)
    return pl.pallas_call(
        kernel,
        out_shape=pltpu.VMEM((128, HEADS, VHD), bf16),
        in_specs=[any_spec] * 6,
        out_specs=pl.BlockSpec(memory_space=pltpu.VMEM),
        scratch_shapes=[
            pltpu.VMEM((32, 32), jnp.int32),
            pltpu.VMEM((32, 32), jnp.int32),
            pltpu.VMEM((40, 128), jnp.int32),
            pltpu.SMEM((40, 128), jnp.int32),
            pltpu.VMEM((128 * HEADS, VHD), jnp.float32),
            pltpu.VMEM((64, BLK, HALF), bf16),
            pltpu.VMEM((64, 2048), bf16),
            pltpu.VMEM((1024, 128), jnp.float32),
            pltpu.VMEM((64, 16, 128), bf16),
            pltpu.VMEM((3, PICKS, BLK, 128), jnp.float32),
            pltpu.VMEM((HEADS, NOPE, KVL), bf16),
            pltpu.VMEM((HEADS, KVL, VHD), bf16),
            pltpu.VMEM((8, N_HEAD * HEAD_COLS), bf16),
            pltpu.VMEM((2, 512, KVL + 128), bf16),
            pltpu.VMEM((2, 512, KVL), jnp.float32),
            pltpu.VMEM((2, 512, 128), jnp.float32),
            pltpu.VMEM((2, 512, 128), jnp.float32),
            pltpu.VMEM((CLASSES, PICKS, SLOT, 128), bf16),
            pltpu.VMEM((CLASSES, PICKS, SLOT, 128), bf16),
        ]
        + [pltpu.VMEM((N_CTX, SLOT, 128), bf16)] * (2 * nd)
        + [
            dma((9,)),
            dma((N_HEAD,)),
            dma((N_HEAD,)),
            dma((nd, N_CTX)),
            dma((nd, N_CTX)),
            dma((2, RING_STEPS, SUBS)),
            dma((2, RING_STEPS, SUBS)),
            dma((SUBS,)),
            dma((SUBS,)),
            dma((CLASSES, SUBS)),
            dma((CLASSES, SUBS)),
        ],
        compiler_params=pltpu.CompilerParams(
            collective_id=0, has_side_effects=True, vmem_limit_bytes=62 * 1024 * 1024
        ),
    )(queries, cache_latent, cache_rope, selected, w_uk, value_up_weight)


def solution(mesh):
    placed = (
        P(("ctx", "head"), None),
        P("ctx", None, None),
        P("ctx", None),
        P(),
        P("head", None, None),
        P("head", None, None),
    )
    return jax.shard_map(
        local, mesh=mesh, in_specs=placed, out_specs=P("ctx", "head", None), check_vma=False
    )
```

time: 770 us -> 47.8 us (0.06)
  waiting for transfers between devices: 327 us -> 0 us
  matrix products: 180 us -> 0 us
  local copies, waits for them, and re-layouts: 99.3 us -> 0.71 us
  blocking collectives: 89 us -> 0 us
  other arithmetic: 55.6 us -> 0 us
  Pallas kernels: 0 us -> 47 us
  between operations: 13.3 us -> 0.01 us
    dot_general x161 -> x0, matrix products: 180 us -> none  [the longest x32 61.8 us: score_rows(): jnp.einsum('rhe,te->rht', block_rope, rope_rows, preferred_element_type=j...]
    reduce_scatter x2 -> x0, waiting for transfers between devices: 178 us -> none  [the longest x1 93.1 us: local(): lax.psum_scatter(partial_values.reshape(all_rows, head_count, VHD), 'ctx'...]
    all_gather x2 -> x0, waiting for transfers between devices: 148 us -> none  [the longest x1 122 us: local(): lax.all_gather(latent_query, 'ctx', axis=0, tiled=True)]
    pmax x1 -> x0, blocking collectives: 64.3 us -> none  [local(): lax.pmax(local_top.astype(jnp.bfloat16), 'ctx').astype(local_top.dtype)]
    dynamic_update_slice x64 -> x0, local copies, waits for them, and re-layouts: 47.3 us -> none  [local(): lax.map(mix_block, (scores, row_top, latent_here, keep_mask))]
    pallas_call x0 -> x1, Pallas kernels: none -> 47 us  [local(): pl.pallas_call(kernel, out_shape=pltpu.VMEM((128, HEADS, VHD), bf16), in_...]
    reduce_sum x34 -> x0, other arithmetic: 43.7 us -> none  [the longest x32 40.6 us: mix_block(): jnp.sum(weights, axis=2)]
    all_to_all x1 -> x0, blocking collectives: 24.7 us -> none  [local(): lax.all_to_all(queries, 'head', split_axis=1, concat_axis=0, tiled=True)]
  transfers between devices with their start and end apart: 4 -> 0, of which waited for: 4 -> 0; matrix products, arithmetic and copies ran while one was open for 4% -> 0% of each run, Pallas kernels for 0% -> 0%
where the time goes in v1:
time: 47.8 us; the launch traced here: 47.7 us
  Pallas kernels  47 us (98%)
  local copies, waits for them, and re-layouts  0.71 us (1%)
    pallas_call x1, Pallas kernels, local(): pl.pallas_call(kernel, out_shape=pltpu.VMEM((128, HEADS, VHD), bf16), in_...  47 us

profile of v1, /device:TPU:1, one launch (start us, length us, event | category | flops | bytes accessed | tf_op | source)
XLA Modules:
  0.0 47.7 jit_solution(8882598993851930728)
XLA Ops:
  0.0 47.0 %shard_map.64 = bf16[128,8,128]{2,1,0:T(8,128)(2,1)S(1)} custom-call(bf16[8,24576]{1,0:T(8,128)(2,1)} %q_hbm.1, bf16[64,64,512]{2,1,0:T(8,128)(2,1)} %cache_hbm.1, bf16[64,4096]{1,0:T(8,128)(2,1)} %rope_hbm.1, s32[32,32]{1,0:T(8,128)} %sel_hbm.1, bf16[8,128,512]{2,1,0:T(8,128)(2,1)} %w_hbm.1, bf16[8,512,128]{2,1,0:T(8,128)(2,1)} %v_hbm.1), custom_call_target="tpu_custom_call" | custom-call | tf_op jit(solution)/shard_map/pallas_call | solution.py:451
  47.0 0.7 %copy.8 = bf16[128,8,128]{2,1,0:T(8,128)(2,1)} copy(bf16[128,8,128]{2,1,0:T(8,128)(2,1)S(1)} %shard_map.64) | data formatting | bytes 524288

commit v2 on v1

--- a/solution.py
+++ b/solution.py
@@ -26,12 +26,16 @@
 RING_STEPS = 2
 SUBS = 2
 SUB = PICKS // SUBS
-NT = (((1,), (1,)), ((), ()))
-ROW_TILE = 256
 SCALE = math.log2(math.e) / math.sqrt(NOPE + ROPE)
 
 
-def kernel(
+def kernel(*refs):
+    spaces = [pltpu.ACC(t)((256, 256), jnp.float32) for t in (0, 0, 1, 1)] * 2
+    pl.run_scoped(lambda *accumulators: body(accumulators, *refs), *spaces)
+
+
+def body(
+    accumulators,
     q_hbm,
     cache_hbm,
     rope_hbm,
@@ -61,6 +65,7 @@
     *rest,
 ):
     nd = len(DIRECT)
+    score_acc, mix_acc = accumulators[:4], accumulators[4:]
     send_bufs, recv_bufs = rest[:nd], rest[nd : 2 * nd]
     (
         local_sem,
@@ -223,6 +228,7 @@
     acc[...] = jnp.zeros_like(acc)
     total[...] = jnp.zeros_like(total)
     top[...] = jnp.full_like(top, -1e30)
+    q_all[:, :, KVL + 128 :] = jnp.zeros((2, 512, 128), jnp.bfloat16)
 
     def ring_copy(direction, step, sub):
         source = (CLASSES - step) % CLASSES if direction == 0 else step
@@ -284,60 +290,74 @@
         for j in range(PICKS):
             g_mine[rel, j] = recv_bufs[d][tab[row, lax.rem(group, 4) + 4 * j]]
 
-    def load(rel, first, count, place):
-        picks = pl.ds(first, count)
-        latent = jnp.concatenate(
-            [
-                g_mine[rel, picks, 0:64, :],
-                g_mine[rel, picks, 64:128, :],
-                g_other[rel, picks, 0:64, :],
-                g_other[rel, picks, 64:128, :],
-            ],
-            axis=2,
-        ).reshape(count * BLK, KVL)
-        lane_low = lax.broadcasted_iota(jnp.int32, (count, 16, 128), 2) < 64
+    lane_low = lax.broadcasted_iota(jnp.int32, (SUB, 16, 128), 2) < 64
+    blank = jnp.zeros((SUB * BLK, 128), jnp.bfloat16)
+
+    def load(rel, sub, place):
+        picks = pl.ds(sub * SUB, SUB)
+        found = []
         for held, half in ((g_mine, core), (g_other, 1 - core)):
+            found.append(
+                jnp.concatenate(
+                    [held[rel, picks, 0:64, :], held[rel, picks, 64:128, :]], axis=2
+                ).reshape(SUB * BLK, HALF)
+            )
             pairs = held[rel, picks, 128:144, :].astype(jnp.float32)
             zero = jnp.zeros_like(pairs)
             even = pl.ds(32 * half, 16, stride=2)
             odd = pl.ds(32 * half + 1, 16, stride=2)
-            rope_keys[place, 0:count, even, :] = jnp.where(lane_low, pairs, zero)
-            rope_keys[place, 0:count, odd, :] = jnp.where(lane_low, zero, pairs)
-        rope = rope_keys[place, 0:count].astype(jnp.bfloat16).reshape(count * BLK, 128)
-        return latent, jnp.concatenate([latent, rope], axis=1)
+            rope_keys[place, :, even, :] = jnp.where(lane_low, pairs, zero)
+            rope_keys[place, :, odd, :] = jnp.where(lane_low, zero, pairs)
+        rope = rope_keys[place].astype(jnp.bfloat16).reshape(SUB * BLK, 128)
+        found.append(jnp.concatenate([rope, blank], axis=1))
+        return found
 
     def attend(*items):
-        for rel, first, count in items:
-            for sub in range(first // SUB, (first + count) // SUB):
-                core_copy(rel, sub).wait_recv()
-        units = []
-        for place, (rel, first, count) in enumerate(items):
-            b = lax.div(lax.rem(z + rel, CLASSES), 4)
-            latent, keys = load(rel, first, count, place)
-            for tile in range(512 // ROW_TILE):
-                units.append((b, pl.ds(tile * ROW_TILE, ROW_TILE), latent, keys))
-
-        def score_unit(b, rows, _, keys):
-            return lax.dot_general(q_all[b, rows, :], keys, NT, preferred_element_type=jnp.float32)
-
-        score = score_unit(*units[0])
-        for place, (b, rows, latent, keys) in enumerate(units):
-            later = score_unit(*units[place + 1]) if place + 1 < len(units) else None
-            before = top[b, rows, :]
-            now = jnp.maximum(before, jnp.max(score, axis=1, keepdims=True))
-            fade = jnp.exp2((before - now) * SCALE)
-            parts = [
-                jnp.exp2((score[:, c * 128 : c * 128 + 128] - now) * SCALE)
-                for c in range(score.shape[1] // 128)
-            ]
-            top[b, rows, :] = now
-            total[b, rows, :] = total[b, rows, :] * fade + sum(parts[1:], parts[0])
-            weights = jnp.concatenate(parts, axis=1).astype(jnp.bfloat16)
-            mixed = jnp.dot(weights, latent, preferred_element_type=jnp.float32)
-            for c in range(4):
-                cols = slice(c * 128, c * 128 + 128)
-                acc[b, rows, cols] = acc[b, rows, cols] * fade + mixed[:, cols]
-            score = later
+        for rel, sub in items:
+            core_copy(rel, sub).wait_recv()
+        groups = [lax.div(lax.rem(z + rel, CLASSES), 4) for rel, _ in items]
+        loaded = [load(rel, sub, place) for place, (rel, sub) in enumerate(items)]
+
+        def score(place):
+            for k in range(3):
+                for t in range(2):
+                    pltpu.matmul_push_rhs(loaded[place][k], k % 2, t, transpose=True)
+                    pltpu.matmul_acc_lhs(
+                        score_acc[2 * t + place % 2],
+                        q_all[groups[place], t * 256 : t * 256 + 256, k * 256 : k * 256 + 256],
+                        load_staged_rhs=k % 2,
+                    )
+
+        score(0)
+        for place, b in enumerate(groups):
+            if place + 1 < len(items):
+                score(place + 1)
+            fades = []
+            for t in range(2):
+                rows = slice(t * 256, t * 256 + 256)
+                scores = pltpu.matmul_pop(score_acc[2 * t + place % 2])
+                before = top[b, rows, :]
+                now = jnp.maximum(before, jnp.max(scores, axis=1, keepdims=True))
+                fade = jnp.exp2((before - now) * SCALE)
+                parts = [
+                    jnp.exp2((scores[:, c * 128 : c * 128 + 128] - now) * SCALE) for c in range(2)
+                ]
+                top[b, rows, :] = now
+                total[b, rows, :] = total[b, rows, :] * fade + (parts[0] + parts[1])
+                weights = jnp.concatenate(parts, axis=1).astype(jnp.bfloat16)
+                fades.append(fade)
+                for n in range(2):
+                    pltpu.matmul_push_rhs(loaded[place][n], n, t)
+                    pltpu.matmul_acc_lhs(mix_acc[2 * t + n], weights, load_staged_rhs=n)
+            for t in range(2):
+                rows = slice(t * 256, t * 256 + 256)
+                for n in range(2):
+                    mixed = pltpu.matmul_pop(mix_acc[2 * t + n])
+                    for c in range(2):
+                        cols = slice(n * 256 + c * 128, n * 256 + c * 128 + 128)
+                        acc[b, rows, cols] = (
+                            acc[b, rows, cols] * fades[t] + mixed[:, c * 128 : c * 128 + 128]
+                        )
 
     def forward(step, sub):
         for direction in range(2):
@@ -382,15 +402,31 @@
             swap2 = pltpu.roll(tiles[2], 64, 1)
             nopes = (tiles[0], jnp.where(low, swap1, swap2))
             ropes = (jnp.where(low, tiles[1], swap1), jnp.where(low, swap2, tiles[2]))
+            blank = jnp.zeros((128, 128), jnp.bfloat16)
+            left = jnp.concatenate(
+                [
+                    jnp.concatenate([nopes[0].astype(jnp.bfloat16), blank], axis=1),
+                    jnp.concatenate([blank, nopes[1].astype(jnp.bfloat16)], axis=1),
+                ],
+                axis=0,
+            )
+            for t in range(2):
+                right = w_v[2 * pair : 2 * pair + 2, :, t * 256 : t * 256 + 256]
+                pltpu.matmul_push_rhs(right.reshape(256, 256), 0, t)
+                pltpu.matmul_acc_lhs(score_acc[2 * t + pair % 2], left, load_staged_rhs=0)
+            for t in range(2):
+                absorbed = pltpu.matmul_pop(score_acc[2 * t + pair % 2]).astype(jnp.bfloat16)
+                for parity in range(2):
+                    start = (2 * pair + parity) * 64
+                    for b in range(2):
+                        q_all[b, start : start + 64, t * 256 : t * 256 + 256] = absorbed[
+                            parity * 128 + b * 64 : parity * 128 + b * 64 + 64
+                        ]
             for parity in range(2):
-                n = 2 * pair + parity
-                absorbed = jnp.dot(
-                    nopes[parity].astype(jnp.bfloat16), w_v[n], preferred_element_type=jnp.float32
-                ).astype(jnp.bfloat16)
+                start = (2 * pair + parity) * 64
                 rope = ropes[parity].astype(jnp.bfloat16)
                 for b in range(2):
-                    q_all[b, n * 64 : n * 64 + 64, 0:KVL] = absorbed[b * 64 : b * 64 + 64]
-                    q_all[b, n * 64 : n * 64 + 64, KVL:] = rope[b * 64 : b * 64 + 64]
+                    q_all[b, start : start + 64, KVL : KVL + 128] = rope[b * 64 : b * 64 + 64]
 
     take(0)
     for sub in range(SUBS):
@@ -399,32 +435,48 @@
     share(0)
     give(2)
     absorb()
-    attend((0, 0, PICKS))
+    attend((0, 0), (0, 1))
     forward(0, 0)
-    attend((7, 0, SUB), (1, 0, SUB))
+    attend((7, 0), (1, 0))
     forward(0, 1)
     take(1)
     share(4)
-    attend((7, SUB, SUB), (1, SUB, SUB))
+    attend((7, 1), (1, 1))
     forward(1, 0)
-    attend((4, 0, PICKS), (6, 0, SUB), (2, 0, SUB))
+    attend((4, 0), (4, 1), (6, 0), (2, 0))
     forward(1, 1)
     take(2)
     share(direct(2))
-    attend((6, SUB, SUB), (2, SUB, SUB))
+    attend((6, 1), (2, 1))
     end(0)
-    attend((direct(2), 0, SUB), (last, 0, SUB))
+    attend((direct(2), 0), (last, 0))
     end(1)
-    attend((direct(2), SUB, SUB), (last, SUB, SUB))
+    attend((direct(2), 1), (last, 1))
 
     copies[5].wait()
     copies[6].wait()
-    for n in range(HEADS):
-        rows = slice(n * 64, n * 64 + 64)
-        mixed = acc[:, rows, :].reshape(128, KVL).astype(jnp.bfloat16)
-        value = jnp.dot(mixed, v_v[n], preferred_element_type=jnp.float32)
-        sums = jnp.sum(total[:, rows, :].reshape(128, 128), axis=1, keepdims=True)
-        out_wide[pl.ds(n, 128, stride=HEADS), :] = value / sums
+    for pair in range(HEADS // 2):
+        t = pair % 2
+        rows = slice(pair * 128, pair * 128 + 128)
+        for k in range(2):
+            deep = slice(k * 256, k * 256 + 256)
+            right = jnp.concatenate([v_v[2 * pair, deep, :], v_v[2 * pair + 1, deep, :]], axis=1)
+            left = acc[:, rows, deep].reshape(256, 256).astype(jnp.bfloat16)
+            pltpu.matmul_push_rhs(right, k, t)
+            pltpu.matmul_acc_lhs(mix_acc[2 * t + pair // 2], left, load_staged_rhs=k)
+    for pair in range(HEADS // 2):
+        value = pltpu.matmul_pop(mix_acc[2 * (pair % 2) + pair // 2])
+        sums = jnp.sum(
+            total[:, pair * 128 : pair * 128 + 128, :].reshape(256, 128), axis=1, keepdims=True
+        )
+        for parity in range(2):
+            parts = []
+            for b in range(2):
+                rows = slice(b * 128 + parity * 64, b * 128 + parity * 64 + 64)
+                parts.append(value[rows, parity * 128 : parity * 128 + 128] / sums[rows])
+            out_wide[pl.ds(2 * pair + parity, 128, stride=HEADS), :] = jnp.concatenate(
+                parts, axis=0
+            )
     out[...] = out_wide[...].astype(jnp.bfloat16).reshape(128, HEADS, VHD)
 
     @pl.loop(1, N_HEAD)
@@ -463,11 +515,11 @@
             pltpu.VMEM((64, 2048), bf16),
             pltpu.VMEM((1024, 128), jnp.float32),
             pltpu.VMEM((64, 16, 128), bf16),
-            pltpu.VMEM((3, PICKS, BLK, 128), jnp.float32),
+            pltpu.VMEM((4, SUB, BLK, 128), jnp.float32),
             pltpu.VMEM((HEADS, NOPE, KVL), bf16),
             pltpu.VMEM((HEADS, KVL, VHD), bf16),
             pltpu.VMEM((8, N_HEAD * HEAD_COLS), bf16),
-            pltpu.VMEM((2, 512, KVL + 128), bf16),
+            pltpu.VMEM((2, 512, KVL + 256), bf16),
             pltpu.VMEM((2, 512, KVL), jnp.float32),
             pltpu.VMEM((2, 512, 128), jnp.float32),
             pltpu.VMEM((2, 512, 128), jnp.float32),

time: 47.8 us -> 47.9 us (level)
  no operation moved by 1% of the time
where the time goes in v2:
time: 47.9 us; the launch traced here: 47.8 us
  Pallas kernels  47 us (98%)
  local copies, waits for them, and re-layouts  0.71 us (1%)
    pallas_call x1, Pallas kernels, local(): pl.pallas_call(kernel, out_shape=pltpu.VMEM((128, HEADS, VHD), bf16), in_...  47 us

profile of v2, /device:TPU:1, one launch (start us, length us, event | category | flops | bytes accessed | tf_op | source)
XLA Modules:
  0.0 47.8 jit_solution(9932431562857307434)
XLA Ops:
  0.0 47.0 %shard_map.64 = bf16[128,8,128]{2,1,0:T(8,128)(2,1)S(1)} custom-call(bf16[8,24576]{1,0:T(8,128)(2,1)} %refs_0_.1, bf16[64,64,512]{2,1,0:T(8,128)(2,1)} %refs_1_.1, bf16[64,4096]{1,0:T(8,128)(2,1)} %refs_2_.1, s32[32,32]{1,0:T(8,128)} %refs_3_.1, bf16[8,128,512]{2,1,0:T(8,128)(2,1)} %refs_4_.1, bf16[8,512,128]{2,1,0:T(8,128)(2,1)} %refs_5_.1), custom_call_target="tpu_custom_call" | custom-call | tf_op jit(solution)/shard_map/pallas_call | solution.py:503
  47.1 0.7 %copy.8 = bf16[128,8,128]{2,1,0:T(8,128)(2,1)} copy(bf16[128,8,128]{2,1,0:T(8,128)(2,1)S(1)} %shard_map.64) | data formatting | bytes 524288

commit v3 on v2

--- a/solution.py
+++ b/solution.py
@@ -26,11 +26,15 @@
 RING_STEPS = 2
 SUBS = 2
 SUB = PICKS // SUBS
+PIECE = 64
+PIECES = 256 // PIECE
 SCALE = math.log2(math.e) / math.sqrt(NOPE + ROPE)
 
 
 def kernel(*refs):
-    spaces = [pltpu.ACC(t)((256, 256), jnp.float32) for t in (0, 0, 1, 1)] * 2
+    spaces = [
+        pltpu.ACC(t)((PIECE, 256), jnp.float32) for t in (0, 0, 1, 1) for _ in range(PIECES)
+    ] * 2
     pl.run_scoped(lambda *accumulators: body(accumulators, *refs), *spaces)
 
 
@@ -65,7 +69,20 @@
     *rest,
 ):
     nd = len(DIRECT)
-    score_acc, mix_acc = accumulators[:4], accumulators[4:]
+    sets = [accumulators[i : i + PIECES] for i in range(0, 8 * PIECES, PIECES)]
+    score_acc, mix_acc = sets[:4], sets[4:]
+
+    def multiply(target, left, staged):
+        for piece in range(PIECES):
+            pltpu.matmul_acc_lhs(
+                target[piece],
+                left(piece * PIECE),
+                load_staged_rhs=staged if piece == 0 else None,
+            )
+
+    def pop(target):
+        return jnp.concatenate([pltpu.matmul_pop(piece) for piece in target], axis=0)
+
     send_bufs, recv_bufs = rest[:nd], rest[nd : 2 * nd]
     (
         local_sem,
@@ -163,7 +180,7 @@
     tab_copy.start()
 
     def q_copy(i):
-        to = lax.rem(head + i, N_HEAD)
+        to = 2 * lax.rem(z + 3 * i, 8) + lax.rem(core + lax.div(i, 8), 2)
         return pltpu.make_async_remote_copy(
             src_ref=q_hbm.at[:, pl.ds(pl.multiple_of(to * HEAD_COLS, 128), HEAD_COLS)],
             dst_ref=q_land.at[:, pl.ds(pl.multiple_of(head * HEAD_COLS, 128), HEAD_COLS)],
@@ -173,13 +190,18 @@
             device_id_type=MESH,
         )
 
+    def partner(i):
+        offset = lax.rem(7 * i, N_CTX)
+        row = lax.rem(lax.div(ctx, 4) + lax.div(offset, 4), 4)
+        return 4 * row + lax.rem(lax.rem(ctx, 4) + lax.rem(offset, 4), 4)
+
     def xy_copy(d, i):
         return pltpu.make_async_remote_copy(
             src_ref=send_bufs[d].at[i],
             dst_ref=recv_bufs[d].at[ctx],
             send_sem=xy_send.at[d, i],
             recv_sem=xy_recv.at[d, i],
-            device_id={"ctx": lax.rem(ctx + i, N_CTX), "head": head},
+            device_id={"ctx": partner(i), "head": head},
             device_id_type=MESH,
         )
 
@@ -191,7 +213,7 @@
     def stage(d):
         @pl.loop(1, N_CTX, unroll=5)
         def _(i):
-            latent, rope = picked(d, lax.rem(ctx + i, N_CTX))
+            latent, rope = picked(d, partner(i))
             send_bufs[d][i, 0:64, :] = latent[:, :128]
             send_bufs[d][i, 64:128, :] = latent[:, 128:]
             send_bufs[d][i, 128:144, :] = rope
@@ -207,10 +229,6 @@
             xy_copy(d, i).start()
 
     pl.semaphore_wait(barrier, 2 * (N_CTX - 1))
-
-    @pl.loop(1, N_HEAD)
-    def _(i):
-        q_copy(i).start()
 
     copies[1].wait()
     for i in range(16):
@@ -222,6 +240,11 @@
     tab_copy.wait()
     stage(0)
     give(0)
+
+    @pl.loop(1, N_HEAD)
+    def _(i):
+        q_copy(i).start()
+
     for d in range(1, nd):
         stage(d)
 
@@ -319,13 +342,18 @@
         loaded = [load(rel, sub, place) for place, (rel, sub) in enumerate(items)]
 
         def score(place):
+            b = groups[place]
             for k in range(3):
                 for t in range(2):
                     pltpu.matmul_push_rhs(loaded[place][k], k % 2, t, transpose=True)
-                    pltpu.matmul_acc_lhs(
+                    multiply(
                         score_acc[2 * t + place % 2],
-                        q_all[groups[place], t * 256 : t * 256 + 256, k * 256 : k * 256 + 256],
-                        load_staged_rhs=k % 2,
+                        lambda first: q_all[
+                            b,
+                            t * 256 + first : t * 256 + first + PIECE,
+                            k * 256 : k * 256 + 256,
+                        ],
+                        k % 2,
                     )
 
         score(0)
@@ -334,30 +362,35 @@
                 score(place + 1)
             fades = []
             for t in range(2):
-                rows = slice(t * 256, t * 256 + 256)
-                scores = pltpu.matmul_pop(score_acc[2 * t + place % 2])
-                before = top[b, rows, :]
-                now = jnp.maximum(before, jnp.max(scores, axis=1, keepdims=True))
-                fade = jnp.exp2((before - now) * SCALE)
-                parts = [
-                    jnp.exp2((scores[:, c * 128 : c * 128 + 128] - now) * SCALE) for c in range(2)
-                ]
-                top[b, rows, :] = now
-                total[b, rows, :] = total[b, rows, :] * fade + (parts[0] + parts[1])
-                weights = jnp.concatenate(parts, axis=1).astype(jnp.bfloat16)
-                fades.append(fade)
+                weights = []
+                for piece in range(PIECES):
+                    rows = slice(t * 256 + piece * PIECE, t * 256 + piece * PIECE + PIECE)
+                    scores = pltpu.matmul_pop(score_acc[2 * t + place % 2][piece])
+                    before = top[b, rows, :]
+                    now = jnp.maximum(before, jnp.max(scores, axis=1, keepdims=True))
+                    fade = jnp.exp2((before - now) * SCALE)
+                    parts = [
+                        jnp.exp2((scores[:, c * 128 : c * 128 + 128] - now) * SCALE)
+                        for c in range(2)
+                    ]
+                    top[b, rows, :] = now
+                    total[b, rows, :] = total[b, rows, :] * fade + (parts[0] + parts[1])
+                    weights.append(jnp.concatenate(parts, axis=1).astype(jnp.bfloat16))
+                    fades.append(fade)
                 for n in range(2):
                     pltpu.matmul_push_rhs(loaded[place][n], n, t)
-                    pltpu.matmul_acc_lhs(mix_acc[2 * t + n], weights, load_staged_rhs=n)
+                    multiply(mix_acc[2 * t + n], lambda first: weights[first // PIECE], n)
             for t in range(2):
-                rows = slice(t * 256, t * 256 + 256)
-                for n in range(2):
-                    mixed = pltpu.matmul_pop(mix_acc[2 * t + n])
-                    for c in range(2):
-                        cols = slice(n * 256 + c * 128, n * 256 + c * 128 + 128)
-                        acc[b, rows, cols] = (
-                            acc[b, rows, cols] * fades[t] + mixed[:, c * 128 : c * 128 + 128]
-                        )
+                for piece in range(PIECES):
+                    rows = slice(t * 256 + piece * PIECE, t * 256 + piece * PIECE + PIECE)
+                    fade = fades[t * PIECES + piece]
+                    for n in range(2):
+                        mixed = pltpu.matmul_pop(mix_acc[2 * t + n][piece])
+                        for c in range(2):
+                            cols = slice(n * 256 + c * 128, n * 256 + c * 128 + 128)
+                            acc[b, rows, cols] = (
+                                acc[b, rows, cols] * fade + mixed[:, c * 128 : c * 128 + 128]
+                            )
 
     def forward(step, sub):
         for direction in range(2):
@@ -413,9 +446,9 @@
             for t in range(2):
                 right = w_v[2 * pair : 2 * pair + 2, :, t * 256 : t * 256 + 256]
                 pltpu.matmul_push_rhs(right.reshape(256, 256), 0, t)
-                pltpu.matmul_acc_lhs(score_acc[2 * t + pair % 2], left, load_staged_rhs=0)
+                multiply(score_acc[2 * t + pair % 2], lambda first: left[first : first + PIECE], 0)
             for t in range(2):
-                absorbed = pltpu.matmul_pop(score_acc[2 * t + pair % 2]).astype(jnp.bfloat16)
+                absorbed = pop(score_acc[2 * t + pair % 2]).astype(jnp.bfloat16)
                 for parity in range(2):
                     start = (2 * pair + parity) * 64
                     for b in range(2):
@@ -450,6 +483,22 @@
     attend((6, 1), (2, 1))
     end(0)
     attend((direct(2), 0), (last, 0))
+
+    @pl.loop(1, N_HEAD)
+    def _(i):
+        q_copy(i).wait_send()
+        for d in range(nd):
+            xy_copy(d, i).wait_send()
+
+    for step in range(RING_STEPS):
+        for sub in range(SUBS):
+            for direction in range(2):
+                ring_copy(direction, step, sub).wait_send()
+    last_copy(0).wait_send()
+    core_copy(last, 0).wait_send()
+    for rel in (0, 7, 1, 4, 6, 2, direct(2)):
+        for sub in range(SUBS):
+            core_copy(rel, sub).wait_send()
     end(1)
     attend((direct(2), 1), (last, 1))
 
@@ -463,9 +512,9 @@
             right = jnp.concatenate([v_v[2 * pair, deep, :], v_v[2 * pair + 1, deep, :]], axis=1)
             left = acc[:, rows, deep].reshape(256, 256).astype(jnp.bfloat16)
             pltpu.matmul_push_rhs(right, k, t)
-            pltpu.matmul_acc_lhs(mix_acc[2 * t + pair // 2], left, load_staged_rhs=k)
+            multiply(mix_acc[2 * t + pair // 2], lambda first: left[first : first + PIECE], k)
     for pair in range(HEADS // 2):
-        value = pltpu.matmul_pop(mix_acc[2 * (pair % 2) + pair // 2])
+        value = pop(mix_acc[2 * (pair % 2) + pair // 2])
         sums = jnp.sum(
             total[:, pair * 128 : pair * 128 + 128, :].reshape(256, 128), axis=1, keepdims=True
         )
@@ -479,20 +528,8 @@
             )
     out[...] = out_wide[...].astype(jnp.bfloat16).reshape(128, HEADS, VHD)
 
-    @pl.loop(1, N_HEAD)
-    def _(i):
-        q_copy(i).wait_send()
-        for d in range(nd):
-            xy_copy(d, i).wait_send()
-
-    for step in range(RING_STEPS):
-        for sub in range(SUBS):
-            for direction in range(2):
-                ring_copy(direction, step, sub).wait_send()
-    for sub in range(SUBS):
-        last_copy(sub).wait_send()
-        for rel in range(CLASSES):
-            core_copy(rel, sub).wait_send()
+    last_copy(1).wait_send()
+    core_copy(last, 1).wait_send()
 
 
 def local(queries, cache_latent, cache_rope, selected, w_uk, value_up_weight):

time: 47.9 us -> 48.1 us (level)
  no operation moved by 1% of the time
where the time goes in v3:
time: 48.1 us; the launch traced here: 47.9 us
  Pallas kernels  47.2 us (98%)
  local copies, waits for them, and re-layouts  0.71 us (1%)
    pallas_call x1, Pallas kernels, local(): pl.pallas_call(kernel, out_shape=pltpu.VMEM((128, HEADS, VHD), bf16), in_...  47.2 us

profile of v3, /device:TPU:1, one launch (start us, length us, event | category | flops | bytes accessed | tf_op | source)
XLA Modules:
  0.0 47.9 jit_solution(13886368331652807995)
XLA Ops:
  0.0 47.2 %shard_map.64 = bf16[128,8,128]{2,1,0:T(8,128)(2,1)S(1)} custom-call(bf16[8,24576]{1,0:T(8,128)(2,1)} %refs_0_.1, bf16[64,64,512]{2,1,0:T(8,128)(2,1)} %refs_1_.1, bf16[64,4096]{1,0:T(8,128)(2,1)} %refs_2_.1, s32[32,32]{1,0:T(8,128)} %refs_3_.1, bf16[8,128,512]{2,1,0:T(8,128)(2,1)} %refs_4_.1, bf16[8,512,128]{2,1,0:T(8,128)(2,1)} %refs_5_.1), custom_call_target="tpu_custom_call" | custom-call | tf_op jit(solution)/shard_map/pallas_call | solution.py:540
  47.2 0.7 %copy.8 = bf16[128,8,128]{2,1,0:T(8,128)(2,1)} copy(bf16[128,8,128]{2,1,0:T(8,128)(2,1)S(1)} %shard_map.64) | data formatting | bytes 524288

commit v4 on v3

--- a/solution.py
+++ b/solution.py
@@ -19,6 +19,7 @@
 HEADS = 8
 HEAD_COLS = HEADS * (NOPE + ROPE)
 SLOT = 144
+SPLIT = 96
 CLASSES = 8
 PICKS = 8
 MESH = pl.DeviceIdType.MESH
@@ -94,6 +95,8 @@
         ring_recv,
         last_send,
         last_recv,
+        rest_send,
+        rest_recv,
         core_send,
         core_recv,
     ) = rest[2 * nd :]
@@ -196,9 +199,10 @@
         return 4 * row + lax.rem(lax.rem(ctx, 4) + lax.rem(offset, 4), 4)
 
     def xy_copy(d, i):
+        rows = pl.ds(0, SPLIT if d == 2 else SLOT)
         return pltpu.make_async_remote_copy(
-            src_ref=send_bufs[d].at[i],
-            dst_ref=recv_bufs[d].at[ctx],
+            src_ref=send_bufs[d].at[i, rows],
+            dst_ref=recv_bufs[d].at[ctx, rows],
             send_sem=xy_send.at[d, i],
             recv_sem=xy_recv.at[d, i],
             device_id={"ctx": partner(i), "head": head},
@@ -280,6 +284,17 @@
             device_id_type=MESH,
         )
 
+    def rest_copy(sub):
+        part, rows = pl.ds(sub * SUB, SUB), pl.ds(SPLIT, SLOT - SPLIT)
+        return pltpu.make_async_remote_copy(
+            src_ref=g_mine.at[2 + 4 * core, part, rows],
+            dst_ref=g_mine.at[direct(2), part, rows],
+            send_sem=rest_send.at[sub],
+            recv_sem=rest_recv.at[sub],
+            device_id={"ctx": ctx, "head": lax.rem(head + 14 - (N_HEAD - 4) * core, N_HEAD)},
+            device_id_type=MESH,
+        )
+
     def core_copy(rel, sub):
         part = pl.ds(sub * SUB, SUB)
         return pltpu.make_async_remote_copy(
@@ -311,7 +326,11 @@
         group = lax.rem(z + rel, CLASSES)
         row = 32 + lax.div(group, 4)
         for j in range(PICKS):
-            g_mine[rel, j] = recv_bufs[d][tab[row, lax.rem(group, 4) + 4 * j]]
+            source = tab[row, lax.rem(group, 4) + 4 * j]
+            if d == 2:
+                g_mine[rel, j, 0:SPLIT, :] = recv_bufs[d][source, 0:SPLIT, :]
+            else:
+                g_mine[rel, j] = recv_bufs[d][source]
 
     lane_low = lax.broadcasted_iota(jnp.int32, (SUB, 16, 128), 2) < 64
     blank = jnp.zeros((SUB * BLK, 128), jnp.bfloat16)
@@ -399,12 +418,15 @@
                 ring_copy(direction, step + 1, sub).start()
         if step + 1 == RING_STEPS:
             last_copy(sub).start()
+            rest_copy(sub).start()
         for rel in (CLASSES - step - 1, step + 1):
             core_copy(rel, sub).start()
 
     def end(sub):
         last_copy(sub).wait_recv()
         core_copy(last, sub).start()
+        rest_copy(sub).wait_recv()
+        core_copy(direct(2), sub).start()
 
     def absorb():
         copies[2].wait()
@@ -472,15 +494,14 @@
     forward(0, 0)
     attend((7, 0), (1, 0))
     forward(0, 1)
+    attend((7, 1), (1, 1))
+    forward(1, 0)
     take(1)
     share(4)
-    attend((7, 1), (1, 1))
-    forward(1, 0)
-    attend((4, 0), (4, 1), (6, 0), (2, 0))
+    attend((6, 0), (2, 0))
     forward(1, 1)
+    attend((4, 0), (4, 1), (6, 1), (2, 1))
     take(2)
-    share(direct(2))
-    attend((6, 1), (2, 1))
     end(0)
     attend((direct(2), 0), (last, 0))
 
@@ -495,8 +516,10 @@
             for direction in range(2):
                 ring_copy(direction, step, sub).wait_send()
     last_copy(0).wait_send()
+    rest_copy(0).wait_send()
     core_copy(last, 0).wait_send()
-    for rel in (0, 7, 1, 4, 6, 2, direct(2)):
+    core_copy(direct(2), 0).wait_send()
+    for rel in (0, 7, 1, 4, 6, 2):
         for sub in range(SUBS):
             core_copy(rel, sub).wait_send()
     end(1)
@@ -529,7 +552,9 @@
     out[...] = out_wide[...].astype(jnp.bfloat16).reshape(128, HEADS, VHD)
 
     last_copy(1).wait_send()
+    rest_copy(1).wait_send()
     core_copy(last, 1).wait_send()
+    core_copy(direct(2), 1).wait_send()
 
 
 def local(queries, cache_latent, cache_rope, selected, w_uk, value_up_weight):
@@ -574,6 +599,8 @@
             dma((2, RING_STEPS, SUBS)),
             dma((SUBS,)),
             dma((SUBS,)),
+            dma((SUBS,)),
+            dma((SUBS,)),
             dma((CLASSES, SUBS)),
             dma((CLASSES, SUBS)),
         ],

time: 48.1 us -> 48.6 us (1.010)
  Pallas kernels: 47.2 us -> 47.7 us
    pallas_call x1, Pallas kernels: 47.2 us -> 47.7 us  [local(): pl.pallas_call(kernel, out_shape=pltpu.VMEM((128, HEADS, VHD), bf16), in_...]
where the time goes in v4:
time: 48.6 us; the launch traced here: 48.4 us
  Pallas kernels  47.7 us (98%)
  local copies, waits for them, and re-layouts  0.71 us (1%)
    pallas_call x1, Pallas kernels, local(): pl.pallas_call(kernel, out_shape=pltpu.VMEM((128, HEADS, VHD), bf16), in_...  47.7 us

profile of v4, /device:TPU:1, one launch (start us, length us, event | category | flops | bytes accessed | tf_op | source)
XLA Modules:
  0.0 48.4 jit_solution(6915470802270426346)
XLA Ops:
  0.0 47.7 %shard_map.64 = bf16[128,8,128]{2,1,0:T(8,128)(2,1)S(1)} custom-call(bf16[8,24576]{1,0:T(8,128)(2,1)} %refs_0_.1, bf16[64,64,512]{2,1,0:T(8,128)(2,1)} %refs_1_.1, bf16[64,4096]{1,0:T(8,128)(2,1)} %refs_2_.1, s32[32,32]{1,0:T(8,128)} %refs_3_.1, bf16[8,128,512]{2,1,0:T(8,128)(2,1)} %refs_4_.1, bf16[8,512,128]{2,1,0:T(8,128)(2,1)} %refs_5_.1), custom_call_target="tpu_custom_call" | custom-call | tf_op jit(solution)/shard_map/pallas_call | solution.py:565
  47.7 0.7 %copy.8 = bf16[128,8,128]{2,1,0:T(8,128)(2,1)} copy(bf16[128,8,128]{2,1,0:T(8,128)(2,1)S(1)} %shard_map.64) | data formatting | bytes 524288

commit v5 on v3

--- a/solution.py
+++ b/solution.py
@@ -137,7 +137,7 @@
         ]
 
     copies = local_copies()
-    for place in (7, 0, 1, 2, 3, 4, 5, 6):
+    for place in (7, 0, 1):
         copies[place].start()
 
     barrier = pltpu.get_barrier_semaphore()
@@ -156,6 +156,9 @@
             device_id={"ctx": ctx, "head": lax.rem(head + i, N_HEAD)},
             device_id_type=MESH,
         )
+
+    for place in (2, 3, 4, 5, 6):
+        copies[place].start()
 
     copies[7].wait()
     sel = sel_v[...]
@@ -235,7 +238,7 @@
         rope_wide[pl.ds(i, 64, stride=16), :] = rope_land[:, i * 128 : i * 128 + 128].astype(
             jnp.float32
         )
-    rope_v[...] = rope_wide[...].astype(jnp.bfloat16).reshape(64, 16, 128)
+    rope_v[...] = rope_wide[0:1024, :].astype(jnp.bfloat16).reshape(64, 16, 128)
     copies[0].wait()
     tab_copy.wait()
     stage(0)
@@ -331,7 +334,7 @@
             odd = pl.ds(32 * half + 1, 16, stride=2)
             rope_keys[place, :, even, :] = jnp.where(lane_low, pairs, zero)
             rope_keys[place, :, odd, :] = jnp.where(lane_low, zero, pairs)
-        rope = rope_keys[place].astype(jnp.bfloat16).reshape(SUB * BLK, 128)
+        rope = rope_keys[place, :, 0:BLK, :].astype(jnp.bfloat16).reshape(SUB * BLK, 128)
         found.append(jnp.concatenate([rope, blank], axis=1))
         return found
 
@@ -526,7 +529,7 @@
             out_wide[pl.ds(2 * pair + parity, 128, stride=HEADS), :] = jnp.concatenate(
                 parts, axis=0
             )
-    out[...] = out_wide[...].astype(jnp.bfloat16).reshape(128, HEADS, VHD)
+    out[...] = out_wide[0 : 128 * HEADS, :].astype(jnp.bfloat16).reshape(128, HEADS, VHD)
 
     last_copy(1).wait_send()
     core_copy(last, 1).wait_send()
@@ -547,12 +550,12 @@
             pltpu.VMEM((32, 32), jnp.int32),
             pltpu.VMEM((40, 128), jnp.int32),
             pltpu.SMEM((40, 128), jnp.int32),
-            pltpu.VMEM((128 * HEADS, VHD), jnp.float32),
+            pltpu.VMEM((128 * HEADS + HEADS, VHD), jnp.float32),
             pltpu.VMEM((64, BLK, HALF), bf16),
             pltpu.VMEM((64, 2048), bf16),
-            pltpu.VMEM((1024, 128), jnp.float32),
+            pltpu.VMEM((1024 + 16, 128), jnp.float32),
             pltpu.VMEM((64, 16, 128), bf16),
-            pltpu.VMEM((4, SUB, BLK, 128), jnp.float32),
+            pltpu.VMEM((4, SUB, BLK + 8, 128), jnp.float32),
             pltpu.VMEM((HEADS, NOPE, KVL), bf16),
             pltpu.VMEM((HEADS, KVL, VHD), bf16),
             pltpu.VMEM((8, N_HEAD * HEAD_COLS), bf16),

time: 48.1 us -> 47.8 us (level)
  no operation moved by 1% of the time
where the time goes in v5:
time: 47.8 us; the launch traced here: 47.7 us
  Pallas kernels  47 us (98%)
  local copies, waits for them, and re-layouts  0.71 us (1%)
    pallas_call x1, Pallas kernels, local(): pl.pallas_call(kernel, out_shape=pltpu.VMEM((128, HEADS, VHD), bf16), in_...  47 us

profile of v5, /device:TPU:1, one launch (start us, length us, event | category | flops | bytes accessed | tf_op | source)
XLA Modules:
  0.0 47.7 jit_solution(1624487244939350043)
XLA Ops:
  0.0 47.0 %shard_map.64 = bf16[128,8,128]{2,1,0:T(8,128)(2,1)S(1)} custom-call(bf16[8,24576]{1,0:T(8,128)(2,1)} %refs_0_.1, bf16[64,64,512]{2,1,0:T(8,128)(2,1)} %refs_1_.1, bf16[64,4096]{1,0:T(8,128)(2,1)} %refs_2_.1, s32[32,32]{1,0:T(8,128)} %refs_3_.1, bf16[8,128,512]{2,1,0:T(8,128)(2,1)} %refs_4_.1, bf16[8,512,128]{2,1,0:T(8,128)(2,1)} %refs_5_.1), custom_call_target="tpu_custom_call" | custom-call | tf_op jit(solution)/shard_map/pallas_call | solution.py:543
  47.0 0.7 %copy.8 = bf16[128,8,128]{2,1,0:T(8,128)(2,1)} copy(bf16[128,8,128]{2,1,0:T(8,128)(2,1)S(1)} %shard_map.64) | data formatting | bytes 524288
